TPU v7x, 32 devices: a whole 2x2x4 slice. The times are simulated.
32 devices in a mesh: dp: 4 (over z), ctx: 8 (over y, x, core).
Axes of the slice: x: 2, y: 2, z: 4, core: 2. Of those that a mesh axis runs over, the one named last changes fastest.
Arguments:
- hidden_in: bfloat16 [4, 1024, 768], P('dp', 'ctx'), may hold values from -6 to 6
- segment_ids: int32 [4, 1024], P('dp', 'ctx'), may hold values from 0 to 4, as said below
- w_qkv: bfloat16 [768, 2304], P('dp'), may hold values from -0.21875 to 0.21875
- w_out: bfloat16 [768, 768], P('dp'), may hold values from -4 to 4
- w_in: bfloat16 [768, 2304], P('dp'), may hold values from -0.21875 to 0.21875
- w_down: bfloat16 [1152, 768], P('dp'), may hold values from -0.1875 to 0.1875
- gain_attn: bfloat16 [768], P('dp'), may hold values from 0.5 to 1.5
- gain_mlp: bfloat16 [768], P('dp'), may hold values from 0.5 to 1.5
- cotangent: bfloat16 [4, 1024, 768], P('dp', 'ctx'), may hold values from -6 to 6
Outputs:
- output: bfloat16 [4, 1024, 768], P('dp', 'ctx')
- grad_input: float32 [4, 1024, 768], P('dp', 'ctx')
- grad_qkv: float32 [768, 2304], P('dp')
- grad_out: float32 [768, 768], P('dp')
- grad_in: float32 [768, 2304], P('dp')
- grad_down: float32 [1152, 768], P('dp')
- grad_gain_attn: float32 [768], P('dp')
- grad_gain_mlp: float32 [768], P('dp')
Inputs may be any that keep to these rules, and one draw needn't show every extreme that they name: `segment_ids`: ids never fall along a sequence; each sequence holds documents 0 to 4; document 2 begins within the first 128 tokens and ends within the last 128; every other document is shorter than 128 tokens.
All inputs are finite; a program needn't handle non-finite values.
Results may differ from a plain program's by a relative error of at most 0.024.
Values may be sent and summed in bfloat16 or wider, within the bound.
A program may use at most 256 MiB of HBM per device.

v0:
```python
import jax
import jax.numpy as jnp
from jax import lax
from jax.sharding import PartitionSpec as P

HEADS = 12
EPSILON = 1e-05
ROPE_THETA = 160000.0
NEGATIVE = -1e30


def layer_norm(values, gain_row):
    average = jnp.mean(values, axis=-1, keepdims=True)
    centred = values - average
    spread = jnp.mean(centred * centred, axis=-1, keepdims=True)
    return centred * lax.rsqrt(spread + EPSILON) * gain_row


def rope_tables(first_row, row_count, head_size):
    position = (first_row + jnp.arange(row_count, dtype=jnp.int32)).astype(jnp.float32)
    frequency = ROPE_THETA ** (-jnp.arange(0, head_size, 2, dtype=jnp.float32) / head_size)
    angles = position[:, None] * frequency[None, :]
    angles = jnp.concatenate([angles, angles], axis=-1)
    return (jnp.cos(angles)[:, None, :], jnp.sin(angles)[:, None, :])


def rotary(values, cosines, sines):
    half_size = values.shape[-1] // 2
    turned = jnp.concatenate([-values[..., half_size:], values[..., :half_size]], axis=-1)
    return values * cosines + turned * sines


def rotary_back(grads, cosines, sines):
    half_size = grads.shape[-1] // 2
    shifted = grads * sines
    return grads * cosines + jnp.concatenate(
        [shifted[..., half_size:], -shifted[..., :half_size]], axis=-1
    )


def geglu(gate_in, gate_up):
    return jax.nn.gelu(gate_in, approximate=False) * gate_up


def contract_rows(left_side, right_side):
    return lax.dot_general(
        left_side, right_side, (((0,), (0,)), ((), ())), preferred_element_type=jnp.float32
    )


def contract_cols(left_side, right_side):
    return lax.dot_general(
        left_side, right_side, (((1,), (1,)), ((), ())), preferred_element_type=jnp.float32
    )


def local(hidden_in, segment_ids, w_qkv, w_out, w_in, w_down, gain_attn, gain_mlp, cotangent):
    local_rows = hidden_in.shape[1]
    model_width = hidden_in.shape[2]
    head_count = HEADS
    head_size = model_width // head_count
    score_scale = head_size ** (-0.5)
    head_shape = (local_rows, head_count, head_size)
    shards = (w_qkv, w_out, w_in, w_down, gain_attn, gain_mlp)
    qkv_full, out_full, in_full, down_full, attn_scale, mlp_scale = (
        lax.all_gather(shards[0], "dp", axis=0, tiled=True),
        lax.all_gather(shards[1], "dp", axis=0, tiled=True),
        lax.all_gather(shards[2], "dp", axis=0, tiled=True),
        lax.all_gather(shards[3], "dp", axis=0, tiled=True),
        lax.all_gather(shards[4], "dp", axis=0, tiled=True),
        lax.all_gather(shards[5], "dp", axis=0, tiled=True),
    )
    hidden_units = in_full.shape[1] // 2
    source = hidden_in[0].astype(jnp.float32)
    own_ids = segment_ids[0]
    cosines, sines = rope_tables(lax.axis_index("ctx") * local_rows, local_rows, head_size)
    normed_one = layer_norm(source, attn_scale.astype(jnp.float32)).astype(jnp.bfloat16)
    projected = jnp.dot(normed_one, qkv_full, preferred_element_type=jnp.float32)
    queries = rotary(projected[:, :model_width].reshape(head_shape), cosines, sines).astype(
        jnp.bfloat16
    )
    own_keys = rotary(
        projected[:, model_width : 2 * model_width].reshape(head_shape), cosines, sines
    ).astype(jnp.bfloat16)
    value_flat = projected[:, 2 * model_width :].astype(jnp.bfloat16)
    own_values = value_flat.reshape(head_shape)
    key_flat = own_keys.reshape(local_rows, model_width)
    query_flat = queries.reshape(local_rows, model_width)
    highest = jnp.full((head_count, local_rows), NEGATIVE, jnp.float32)
    block_keys = lax.all_gather(key_flat, "ctx", axis=0, tiled=True)
    block_values = lax.all_gather(value_flat, "ctx", axis=0, tiled=True)
    block_ids = lax.all_gather(own_ids, "ctx", axis=0, tiled=True)
    piece_rows = block_keys.shape[0]
    scores = (
        jnp.einsum(
            "qhe,khe->hqk",
            queries,
            block_keys.reshape(piece_rows, head_count, head_size),
            preferred_element_type=jnp.float32,
        )
        * score_scale
    )
    allowed = (own_ids[:, None] == block_ids[None, :])[None]
    scores = jnp.where(allowed, scores, NEGATIVE)
    raised = jnp.maximum(highest, jnp.max(scores, axis=-1))
    weights = jnp.where(allowed, jnp.exp(scores - raised[..., None]), 0.0)
    row_total = jnp.sum(weights, axis=-1)
    update = jnp.einsum(
        "hqk,khe->qhe",
        weights.astype(jnp.bfloat16),
        block_values.reshape(piece_rows, head_count, head_size),
        preferred_element_type=jnp.float32,
    )
    summed = update
    highest, row_total, summed = (raised, row_total, summed)
    attention = summed / jnp.transpose(row_total)[:, :, None]
    log_total = highest + jnp.log(row_total)
    attended = attention.reshape(local_rows, model_width).astype(jnp.bfloat16)
    middle = source + jnp.dot(attended, out_full, preferred_element_type=jnp.float32)
    normed_two = layer_norm(middle, mlp_scale.astype(jnp.float32)).astype(jnp.bfloat16)
    lifted = jnp.dot(normed_two, in_full, preferred_element_type=jnp.float32)
    gate_in = lifted[:, :hidden_units]
    gate_up = lifted[:, hidden_units:]
    mixed_units = geglu(gate_in, gate_up).astype(jnp.bfloat16)
    result = (middle + jnp.dot(mixed_units, down_full, preferred_element_type=jnp.float32)).astype(
        jnp.bfloat16
    )
    qkv_back, out_back, in_back, down_back, attn_back, mlp_back = (
        lax.all_gather(shards[0], "dp", axis=0, tiled=True),
        lax.all_gather(shards[1], "dp", axis=0, tiled=True),
        lax.all_gather(shards[2], "dp", axis=0, tiled=True),
        lax.all_gather(shards[3], "dp", axis=0, tiled=True),
        lax.all_gather(shards[4], "dp", axis=0, tiled=True),
        lax.all_gather(shards[5], "dp", axis=0, tiled=True),
    )
    upstream = cotangent[0]
    grad_down = contract_rows(mixed_units, upstream)
    grad_mixed = contract_cols(upstream, down_back)
    _, pull_gate = jax.vjp(geglu, gate_in, gate_up)
    grad_gate_in, grad_gate_up = pull_gate(grad_mixed)
    grad_lifted = jnp.concatenate([grad_gate_in, grad_gate_up], axis=1).astype(jnp.bfloat16)
    grad_in = contract_rows(normed_two, grad_lifted)
    grad_normed_two = contract_cols(grad_lifted, in_back)
    _, pull_two = jax.vjp(layer_norm, middle, mlp_back.astype(jnp.float32))
    grad_middle_part, grad_mlp_gain = pull_two(grad_normed_two)
    grad_middle = upstream.astype(jnp.float32) + grad_middle_part
    grad_branch = grad_middle.astype(jnp.bfloat16)
    grad_out = contract_rows(attended, grad_branch)
    grad_attended = contract_cols(grad_branch, out_back).astype(jnp.bfloat16)
    grad_heads = grad_attended.reshape(head_shape)
    products = jnp.transpose(jnp.sum(grad_heads.astype(jnp.float32) * attention, axis=-1))
    all_log, all_products, all_ids = (
        lax.all_gather(log_total, "ctx", axis=1, tiled=True),
        lax.all_gather(products, "ctx", axis=1, tiled=True),
        lax.all_gather(own_ids, "ctx", axis=0, tiled=True),
    )
    block_keys = lax.all_gather(key_flat, "ctx", axis=0, tiled=True)
    block_values = lax.all_gather(value_flat, "ctx", axis=0, tiled=True)
    block_ids = lax.all_gather(own_ids, "ctx", axis=0, tiled=True)
    piece_rows = block_keys.shape[0]
    key_heads = block_keys.reshape(piece_rows, head_count, head_size)
    scores = (
        jnp.einsum("qhe,khe->hqk", queries, key_heads, preferred_element_type=jnp.float32)
        * score_scale
    )
    allowed = (own_ids[:, None] == block_ids[None, :])[None]
    probabilities = jnp.where(allowed, jnp.exp(scores - log_total[..., None]), 0.0)
    grad_probs = jnp.einsum(
        "qhe,khe->hqk",
        grad_heads,
        block_values.reshape(piece_rows, head_count, head_size),
        preferred_element_type=jnp.float32,
    )
    grad_scores = (probabilities * (grad_probs - products[..., None])).astype(jnp.bfloat16)
    grad_queries = score_scale * jnp.einsum(
        "hqk,khe->qhe", grad_scores, key_heads, preferred_element_type=jnp.float32
    )
    block_queries = lax.all_gather(query_flat, "ctx", axis=0, tiled=True)
    block_grads = lax.all_gather(grad_attended, "ctx", axis=0, tiled=True)
    piece_rows = block_queries.shape[0]
    query_heads = block_queries.reshape(piece_rows, head_count, head_size)
    grad_rows = block_grads.reshape(piece_rows, head_count, head_size)
    scores = (
        jnp.einsum("qhe,khe->hqk", query_heads, own_keys, preferred_element_type=jnp.float32)
        * score_scale
    )
    allowed = (all_ids[:, None] == own_ids[None, :])[None]
    probabilities = jnp.where(allowed, jnp.exp(scores - all_log[..., None]), 0.0)
    grad_values = jnp.einsum(
        "hqk,qhe->khe",
        probabilities.astype(jnp.bfloat16),
        grad_rows,
        preferred_element_type=jnp.float32,
    )
    grad_probs = jnp.einsum(
        "qhe,khe->hqk", grad_rows, own_values, preferred_element_type=jnp.float32
    )
    grad_scores = (probabilities * (grad_probs - all_products[..., None])).astype(jnp.bfloat16)
    grad_keys = score_scale * jnp.einsum(
        "hqk,qhe->khe", grad_scores, query_heads, preferred_element_type=jnp.float32
    )
    grad_keys, grad_values = (grad_keys, grad_values)
    grad_projected = jnp.concatenate(
        [
            rotary_back(grad_queries, cosines, sines).reshape(local_rows, model_width),
            rotary_back(grad_keys, cosines, sines).reshape(local_rows, model_width),
            grad_values.reshape(local_rows, model_width),
        ],
        axis=1,
    ).astype(jnp.bfloat16)
    grad_qkv = contract_rows(normed_one, grad_projected)
    grad_normed_one = contract_cols(grad_projected, qkv_back)
    _, pull_one = jax.vjp(layer_norm, source, attn_back.astype(jnp.float32))
    grad_source, grad_attn_gain = pull_one(grad_normed_one)
    grad_input = grad_middle + grad_source
    local_grads = (grad_qkv, grad_out, grad_in, grad_down, grad_attn_gain, grad_mlp_gain)
    shares = (
        lax.psum_scatter(
            local_grads[0].astype(jnp.bfloat16), "dp", scatter_dimension=0, tiled=True
        ).astype(jnp.float32),
        lax.psum_scatter(
            local_grads[1].astype(jnp.bfloat16), "dp", scatter_dimension=0, tiled=True
        ).astype(jnp.float32),
        lax.psum_scatter(
            local_grads[2].astype(jnp.bfloat16), "dp", scatter_dimension=0, tiled=True
        ).astype(jnp.float32),
        lax.psum_scatter(
            local_grads[3].astype(jnp.bfloat16), "dp", scatter_dimension=0, tiled=True
        ).astype(jnp.float32),
        lax.psum_scatter(
            local_grads[4].astype(jnp.bfloat16), "dp", scatter_dimension=0, tiled=True
        ).astype(jnp.float32),
        lax.psum_scatter(
            local_grads[5].astype(jnp.bfloat16), "dp", scatter_dimension=0, tiled=True
        ).astype(jnp.float32),
    )
    shares = (
        lax.psum(shares[0].astype(jnp.bfloat16), "ctx").astype(jnp.float32),
        lax.psum(shares[1].astype(jnp.bfloat16), "ctx").astype(jnp.float32),
        lax.psum(shares[2].astype(jnp.bfloat16), "ctx").astype(jnp.float32),
        lax.psum(shares[3].astype(jnp.bfloat16), "ctx").astype(jnp.float32),
        lax.psum(shares[4].astype(jnp.bfloat16), "ctx").astype(jnp.float32),
        lax.psum(shares[5].astype(jnp.bfloat16), "ctx").astype(jnp.float32),
    )
    return (
        result[None],
        grad_input[None],
        shares[0],
        shares[1],
        shares[2],
        shares[3],
        shares[4],
        shares[5],
    )


def solution(mesh):
    in_specs = (
        P("dp", "ctx", None),
        P("dp", "ctx"),
        P("dp", None),
        P("dp", None),
        P("dp", None),
        P("dp", None),
        P("dp"),
        P("dp"),
        P("dp", "ctx", None),
    )
    out_specs = (
        P("dp", "ctx", None),
        P("dp", "ctx", None),
        P("dp", None),
        P("dp", None),
        P("dp", None),
        P("dp", None),
        P("dp"),
        P("dp"),
    )
    return jax.shard_map(local, mesh=mesh, in_specs=in_specs, out_specs=out_specs, check_vma=False)
```

profile of v0, /device:TPU:0, one launch (start us, length us, event | category | flops | bytes accessed | tf_op | source)
XLA Modules:
  0.0 630.1 jit_solution(16062213591360769307)
XLA Ops:
  11.6 13.6 %all-reduce.7 = (bf16[768]{0:T(1024)(128)(2,1)S(1)}, bf16[768]{0:T(1024)(128)(2,1)S(1)}) all-reduce(bf16[768]{0:T(1024)(128)(2,1)S(1)} %dynamic-update-slice, bf16[768]{0:T(1024)(128)(2,1)S(1)} %dynamic-update-slice.1), channel_id=1, replica_groups=mesh['dp'=4,'ctx'=8] {'dp'}, use_global_device_ids=true, to_apply=%add | all-reduce | flops 1536 | bytes 6144
  28.5 53.9 %all-gather.10.cloned.1.call-done = bf16[768,2304]{1,0:T(8,128)(2,1)} async-done(((bf16[192,2304]{1,0:T(8,128)(2,1)}), bf16[768,2304]{1,0:T(8,128)(2,1)}) %all-gather.10.cloned.1.call-update) | async-done | bytes 3538960 | tf_op jit(solution)/shard_map/all_gather | solution.py:66
  92.2 8.7 %all-gather = s32[1,1024]{1,0:T(1,128)S(1)} all-gather(s32[1,128]{1,0:T(1,128)S(1)} %copy-done.44), channel_id=2, replica_groups=mesh['dp'=4,'ctx'=8] {'ctx'}, dimensions={1}, use_global_device_ids=true | all-gather | bytes 4608 | tf_op jit(solution)/shard_map/all_gather | solution.py:92
  101.1 12.9 %all-gather.14.cloned.1.call-done = bf16[1024,768]{1,0:T(8,128)(2,1)} async-done(((bf16[128,768]{1,0:T(8,128)(2,1)}), bf16[1024,768]{1,0:T(8,128)(2,1)}) %all-gather.14.cloned.1.call-update) | async-done | bytes 1572880 | tf_op jit(solution)/shard_map/all_gather | solution.py:90
  121.7 19.9 %all-gather.12.cloned.1.call-done = bf16[1024,768]{1,0:T(8,128)(2,1)} async-done(((bf16[128,768]{1,0:T(8,128)(2,1)}), bf16[1024,768]{1,0:T(8,128)(2,1)}) %all-gather.12.cloned.1.call-update) | async-done | bytes 1572880 | tf_op jit(solution)/shard_map/all_gather | solution.py:91
  144.2 5.8 fusion.88
  150.0 23.5 %all-gather.16.cloned.1.call-done = bf16[768,768]{1,0:T(8,128)(2,1)} async-done(((bf16[192,768]{1,0:T(8,128)(2,1)}), bf16[768,768]{1,0:T(8,128)(2,1)}) %all-gather.16.cloned.1.call-update) | async-done | bytes 1179664 | tf_op jit(solution)/shard_map/all_gather | solution.py:67
  176.0 68.1 %all-gather.18.cloned.1.call-done = bf16[768,2304]{1,0:T(8,128)(2,1)} async-done(((bf16[192,2304]{1,0:T(8,128)(2,1)}), bf16[768,2304]{1,0:T(8,128)(2,1)}) %all-gather.18.cloned.1.call-update) | async-done | bytes 3538960 | tf_op jit(solution)/shard_map/all_gather | solution.py:68
  246.8 37.7 %all-gather.20.cloned.1.call-done = bf16[1152,768]{1,0:T(8,128)(2,1)} async-done(((bf16[288,768]{1,0:T(8,128)(2,1)}), bf16[1152,768]{1,0:T(8,128)(2,1)}) %all-gather.20.cloned.1.call-update) | async-done | bytes 1769488 | tf_op jit(solution)/shard_map/all_gather | solution.py:69
  297.0 3.9 convolution_convert_fusion
  304.5 7.0 %all-gather.22.cloned.1.call-done = bf16[1024,768]{1,0:T(8,128)(2,1)} async-done(((bf16[128,768]{1,0:T(8,128)(2,1)}), bf16[1024,768]{1,0:T(8,128)(2,1)}) %all-gather.22.cloned.1.call-update) | async-done | bytes 1572880 | tf_op jit(solution)/shard_map/all_gather | solution.py:178
  314.8 10.1 %all_gather.59 = f32[12,1024]{1,0:T(8,128)} all-gather(f32[12,128]{1,0:T(8,128)S(1)} %log_add_fusion), channel_id=1, replica_groups=mesh['dp'=4,'ctx'=8] {'ctx'}, dimensions={1}, use_global_device_ids=true | all-gather | bytes 55296 | tf_op jit(solution)/shard_map/all_gather | solution.py:153
  326.0 9.1 %all_gather.61 = f32[12,1024]{1,0:T(8,128)} all-gather(f32[12,128]{1,0:T(8,128)S(1)} %bitcast.131), channel_id=1, replica_groups=mesh['dp'=4,'ctx'=8] {'ctx'}, dimensions={1}, use_global_device_ids=true | all-gather | bytes 55296 | tf_op jit(solution)/shard_map/all_gather | solution.py:154
  335.0 5.2 fusion.54
  343.0 9.0 %fusion.17 = f32[128,12,64]{0,2,1:T(8,128)} fusion(bf16[1024,12,64]{0,2,1:T(8,128)(2,1)} %bitcast.105, f32[12,1024,128]{2,1,0:T(8,128)} %fusion.54, f32[12,1024]{1,0:T(8,128)S(1)} %copy-done.30, f32[12,1024]{1,0:T(8,128)S(1)} %copy-done.28, pred[1024,128]{1,0:T(8,128)(4,1)S(1)} %copy-done.26, bf16[1024,12,64]{0,2,1:T(8,128)(2,1)} %bitcast.114, ...), kind=kOutput, calls=%fused_computation.22 | convolution fusion | flops 412090368 | bytes 10256384 | tf_op jit(solution)/shard_map/hqk,qhe->khe/dot_general | solution.py:199
  352.0 7.1 %broadcast_multiply_fusion.1 = (f32[128,12,64]{0,2,1:T(8,128)}, f32[128,12,64]{0,2,1:T(8,128)S(1)}, f32[128,12,64]{0,2,1:T(8,128)}) fusion(f32[128,64]{0,1:T(8,128)} %get-tuple-element.47, f32[128,12,64]{0,2,1:T(8,128)} %fusion.17, bf16[1024,12,64]{0,2,1:T(8,128)(2,1)S(1)} %bitcast.103, f32[12,128,1024]{2,1,0:T(8,128)} %copy-done, ...), kind=kOutput, calls=%fused_computation.102 | convolution fusion | flops 412286976 | bytes 11382784 | tf_op jit(solution)/shard_map/hqk,khe->qhe/dot_general | solution.py:175
  361.6 5.0 fusion.23
  371.4 39.2 %reduce-scatter.11.cloned.1.call-done = bf16[288,768]{1,0:T(8,128)(2,1)} async-done(((bf16[1152,768]{1,0:T(8,128)(2,1)}), bf16[288,768]{1,0:T(8,128)(2,1)}) %reduce-scatter.11.cloned.1.call-update) | async-done | bytes 442384 | tf_op jit(solution)/shard_map/reduce_scatter | solution.py:227
  410.7 67.9 %reduce-scatter.9.cloned.1.call-done = bf16[192,2304]{1,0:T(8,128)(2,1)} async-done(((bf16[768,2304]{1,0:T(8,128)(2,1)}), bf16[192,2304]{1,0:T(8,128)(2,1)}) %reduce-scatter.9.cloned.1.call-update) | async-done | bytes 884752 | tf_op jit(solution)/shard_map/reduce_scatter | solution.py:224
  478.6 69.0 %reduce-scatter.5.cloned.1.call-done = bf16[192,2304]{1,0:T(8,128)(2,1)} async-done(((bf16[768,2304]{1,0:T(8,128)(2,1)}), bf16[192,2304]{1,0:T(8,128)(2,1)}) %reduce-scatter.5.cloned.1.call-update) | async-done | bytes 884752 | tf_op jit(solution)/shard_map/reduce_scatter | solution.py:218
  548.7 3.5 fusion.47
  552.6 10.7 %all-reduce.6 = (bf16[768]{0:T(1024)(128)(2,1)S(1)}, bf16[768]{0:T(1024)(128)(2,1)S(1)}) all-reduce(bf16[768]{0:T(1024)(128)(2,1)S(1)} %get-tuple-element.10, bf16[768]{0:T(1024)(128)(2,1)S(1)} %copy-done.43), channel_id=7, replica_groups=mesh['dp'=4,'ctx'=8] {'dp'}, use_global_device_ids=true, to_apply=%region_20.21.clone | all-reduce | flops 1536 | bytes 6144
  563.5 12.1 %all-reduce.4 = (bf16[192]{0:T(256)(128)(2,1)S(1)}, bf16[192]{0:T(256)(128)(2,1)S(1)}) all-reduce(bf16[192]{0:T(256)(128)(2,1)S(1)} %dynamic-slice.3, bf16[192]{0:T(256)(128)(2,1)S(1)} %dynamic-slice.5), channel_id=1, replica_groups=mesh['dp'=4,'ctx'=8] {'ctx'}, use_global_device_ids=true, to_apply=%region_21.22 | all-reduce | flops 384 | bytes 1536 | tf_op jit(solution)/shard_map/psum | solution.py:242
  577.7 39.2 %all-reduce.10.cloned.1.call-done = (bf16[192,2304]{1,0:T(8,128)(2,1)}, bf16[192,768]{1,0:T(8,128)(2,1)}, bf16[192,2304]{1,0:T(8,128)(2,1)}, bf16[288,768]{1,0:T(8,128)(2,1)}) async-done(((bf16[192,2304]{1,0:T(8,128)(2,1)}, bf16[192,768]{1,0:T(8,128)(2,1)}, bf16[192,2304]{1,0:T(8,128)(2,1)}, bf16[288,768]{1,0:T(8,128)(2,1)}), (bf16[192,2304]{1,0:T(8,128)(2,1)}, bf16[192,768]{1,0:T(8,128)(2,1)}, ...) | async-done | bytes 2506768 | tf_op jit(solution)/shard_map/psum | solution.py:238
  (202 shorter events, 72.0 us)
Async XLA Ops:
  7.2 75.2 %all-gather.10.cloned.1.call-start = ((), (), s32[]{:S(2)}) async-start(), calls=%async_computation.4 | async-start | bytes 4423680 | tf_op jit(solution)/shard_map/all_gather | solution.py:66
  7.9 106.1 %all-gather.14.cloned.1.call-start = ((), (), s32[]{:S(2)}) async-start(), calls=%async_computation.6 | async-start | bytes 1769472 | tf_op jit(solution)/shard_map/all_gather | solution.py:90
  26.1 89.7 %copy-start.22 = (f32[128,64]{0,1:T(8,128)}, f32[128,64]{0,1:T(8,128)S(1)}, u32[]{:S(2)}) copy-start(f32[128,64]{0,1:T(8,128)S(1)} %get-tuple-element.49) | copy-start | bytes 98308
  27.3 57.9 %copy-start.34 = (f32[128]{0:T(128)}, f32[128]{0:T(128)S(1)}, u32[]{:S(2)}) copy-start(f32[128]{0:T(128)S(1)} %broadcast_multiply_fusion.6) | copy-start | bytes 1540
  28.4 56.8 %copy-start.47 = (f32[128]{0:T(128)}, f32[128]{0:T(128)S(1)}, u32[]{:S(2)}) copy-start(f32[128]{0:T(128)S(1)} %fusion.46) | copy-start | bytes 1540
  28.5 56.8 %copy-start.36 = (f32[128]{0:T(128)}, f32[128]{0:T(128)S(1)}, u32[]{:S(2)}) copy-start(f32[128]{0:T(128)S(1)} %fusion.62) | copy-start | bytes 1540
  89.6 52.1 %all-gather.12.cloned.1.call-start = ((), (), s32[]{:S(2)}) async-start(), calls=%async_computation.5 | async-start | bytes 1769472 | tf_op jit(solution)/shard_map/all_gather | solution.py:91
  90.4 83.2 %all-gather.16.cloned.1.call-start = ((), (), s32[]{:S(2)}) async-start(), calls=%async_computation.7 | async-start | bytes 1474560 | tf_op jit(solution)/shard_map/all_gather | solution.py:67
  90.9 153.2 %all-gather.18.cloned.1.call-start = ((), (), s32[]{:S(2)}) async-start(), calls=%async_computation.8 | async-start | bytes 4423680 | tf_op jit(solution)/shard_map/all_gather | solution.py:68
  91.5 192.9 %all-gather.20.cloned.1.call-start = ((), (), s32[]{:S(2)}) async-start(), calls=%async_computation.9 | async-start | bytes 2211840 | tf_op jit(solution)/shard_map/all_gather | solution.py:69
  92.1 219.4 %all-gather.22.cloned.1.call-start = ((), (), s32[]{:S(2)}) async-start(), calls=%async_computation.10 | async-start | bytes 1769472 | tf_op jit(solution)/shard_map/all_gather | solution.py:178
  101.0 43.2 %copy-start.17 = (pred[128,1024]{1,0:T(8,128)(4,1)}, pred[128,1024]{1,0:T(8,128)(4,1)S(1)}, u32[]{:S(2)}) copy-start(pred[128,1024]{1,0:T(8,128)(4,1)S(1)} %broadcast_compare_fusion.1) | copy-start | bytes 393220
  101.1 239.2 %all-gather.24.cloned.1.call-start = ((), (), s32[]{:S(2)}) async-start(), calls=%async_computation.11 | async-start | bytes 1769472 | tf_op jit(solution)/shard_map/all_gather | solution.py:179
  144.2 29.3 %copy-start.2 = (bf16[1,128,768]{2,1,0:T(8,128)(2,1)S(1)}, bf16[1,128,768]{2,1,0:T(8,128)(2,1)}, u32[]{:S(2)}) copy-start(bf16[1,128,768]{2,1,0:T(8,128)(2,1)} %param.9) | copy-start | bytes 589828
  175.2 109.2 %copy-start.14 = (bf16[1,128,768]{2,1,0:T(8,128)(2,1)S(1)}, bf16[1,128,768]{2,1,0:T(8,128)(2,1)}, u32[]{:S(2)}) copy-start(bf16[1,128,768]{2,1,0:T(8,128)(2,1)} %param.17) | copy-start | bytes 589828
  292.3 79.2 %reduce-scatter.7.cloned.1.call-start = ((), (), s32[]{:S(2)}) async-start(), calls=%async_computation.13 | async-start | bytes 1474560 | tf_op jit(solution)/shard_map/reduce_scatter | solution.py:221
  294.9 115.8 %reduce-scatter.11.cloned.1.call-start = ((), (), s32[]{:S(2)}) async-start(), calls=%async_computation.15 | async-start | bytes 2211840 | tf_op jit(solution)/shard_map/reduce_scatter | solution.py:227
  296.9 181.7 %reduce-scatter.9.cloned.1.call-start = ((), (), s32[]{:S(2)}) async-start(), calls=%async_computation.14 | async-start | bytes 4423680 | tf_op jit(solution)/shard_map/reduce_scatter | solution.py:224
  300.9 34.1 %copy-start.5 = (f32[128,768]{0,1:T(8,128)S(1)}, f32[128,768]{0,1:T(8,128)}, u32[]{:S(2)}) copy-start(f32[128,768]{0,1:T(8,128)} %copy-done.4) | copy-start | bytes 1179652
  300.9 34.1 %copy-start.7 = (f32[128,12,64]{0,2,1:T(8,128)S(1)}, f32[128,12,64]{0,2,1:T(8,128)}, u32[]{:S(2)}) copy-start(f32[128,12,64]{0,2,1:T(8,128)} %copy-done.6) | copy-start | bytes 1179652
  300.9 246.6 %reduce-scatter.5.cloned.1.call-start = ((), (), s32[]{:S(2)}) async-start(), calls=%async_computation.12 | async-start | bytes 4423680 | tf_op jit(solution)/shard_map/reduce_scatter | solution.py:218
  370.3 177.3 %copy-start.11 = (bf16[128,1152]{1,0:T(8,128)(2,1)S(1)}, bf16[128,1152]{1,0:T(8,128)(2,1)}, u32[]{:S(2)}) copy-start(bf16[128,1152]{1,0:T(8,128)(2,1)} %get-tuple-element.27) | copy-start | bytes 884740
  370.3 177.3 %copy-start.13 = (bf16[1152,768]{1,0:T(8,128)(2,1)S(1)}, bf16[1152,768]{1,0:T(8,128)(2,1)}, u32[]{:S(2)}) copy-start(bf16[1152,768]{1,0:T(8,128)(2,1)} %all-gather.20.cloned.1.call-done) | copy-start | bytes 5308420
  370.3 246.5 %all-reduce.10.cloned.1.call-start = ((), (), s32[]{:S(2)}) async-start(), calls=%async_computation.16 | async-start | bytes 5013504 | tf_op jit(solution)/shard_map/psum | solution.py:238
  (40 other events, 256.7 us)
Sparse Core Ops, SparseCore 0:
  9.6 72.7 all-gather.9
  89.7 24.2 all-gather.13
  115.9 25.6 all-gather.11
  143.0 30.4 all-gather.15
  174.9 69.0 all-gather.17
  245.5 38.8 all-gather.19
  286.9 24.5 all-gather.21
  313.4 25.8 all-gather.23
  341.6 29.1 reduce-scatter.6
  373.6 37.0 reduce-scatter.10
  413.1 65.4 reduce-scatter.8
  480.9 66.6 reduce-scatter.4
  551.7 65.0 all-reduce.9
where the time goes:
time: 631 us; the launch traced here: 630 us
  waiting for transfers between devices  441 us (70%)
  blocking collectives  64.3 us (10%)
  matrix products  62.8 us (10%)
  other arithmetic  24.1 us (4%)
  local copies, waits for them, and re-layouts  21.3 us (3%)
  between operations  16 us (3%)
    reduce_scatter x1, waiting for transfers between devices, local(): lax.psum_scatter(local_grads[0].astype(jnp.bfloat16), 'dp', scatter_dimen...  69 us
    all_gather x1, waiting for transfers between devices, local(): lax.all_gather(shards[2], 'dp', axis=0, tiled=True)  68.1 us
    reduce_scatter x1, waiting for transfers between devices, local(): lax.psum_scatter(local_grads[2].astype(jnp.bfloat16), 'dp', scatter_dimen...  67.9 us
    all_gather x1, waiting for transfers between devices, local(): lax.all_gather(shards[0], 'dp', axis=0, tiled=True)  53.9 us
    reduce_scatter x1, waiting for transfers between devices, local(): lax.psum_scatter(local_grads[3].astype(jnp.bfloat16), 'dp', scatter_dimen...  39.2 us
    psum x1, waiting for transfers between devices, local(): lax.psum(shares[0].astype(jnp.bfloat16), 'ctx').astype(jnp.float32)  39.2 us
    all_gather x1, waiting for transfers between devices, local(): lax.all_gather(shards[3], 'dp', axis=0, tiled=True)  37.7 us
    unnamed x2, blocking collectives  24.3 us
  transfers between devices with their start and end apart: 13, of which 11 were waited for; matrix products, arithmetic and copies ran while one was open for 14% of the time, Pallas kernels for 0%

commit v1 on v0

--- a/solution.py
+++ b/solution.py
@@ -7,6 +7,18 @@
 EPSILON = 1e-05
 ROPE_THETA = 160000.0
 NEGATIVE = -1e30
+
+
+def doubled_up(x, axis, dim):
+    ways, here = (lax.axis_size(axis), lax.axis_index(axis))
+    grown, reach = (x, 1)
+    while reach < ways:
+        theirs = lax.ppermute(grown, axis, [(d, d ^ reach) for d in range(ways)])
+        mine_first = jnp.concatenate([grown, theirs], axis=dim)
+        theirs_first = jnp.concatenate([theirs, grown], axis=dim)
+        grown = jnp.where(here & reach == 0, mine_first, theirs_first)
+        reach = 2 * reach
+    return grown
 
 
 def layer_norm(values, gain_row):
@@ -65,7 +77,7 @@
     qkv_full, out_full, in_full, down_full, attn_scale, mlp_scale = (
         lax.all_gather(shards[0], "dp", axis=0, tiled=True),
         lax.all_gather(shards[1], "dp", axis=0, tiled=True),
-        lax.all_gather(shards[2], "dp", axis=0, tiled=True),
+        doubled_up(shards[2], "dp", 0),
         lax.all_gather(shards[3], "dp", axis=0, tiled=True),
         lax.all_gather(shards[4], "dp", axis=0, tiled=True),
         lax.all_gather(shards[5], "dp", axis=0, tiled=True),

time: 631 us -> 658 us (1.043)
  waiting for transfers between devices: 441 us -> 456 us
  matrix products: 62.8 us -> 70.7 us
    ppermute x0 -> x2, waiting for transfers between devices: none -> 67.3 us  [doubled_up(): theirs = lax.ppermute(grown, axis, [(d, d ^ reach) for d in range(ways)])]
    all_gather x1, waiting for transfers between devices: 37.7 us -> 0.02 us  [local(): lax.all_gather(shards[3], 'dp', axis=0, tiled=True)]
    all_gather x1, waiting for transfers between devices: 23.5 us -> 36.7 us  [local(): lax.all_gather(shards[1], 'dp', axis=0, tiled=True)]
    all_gather x1, waiting for transfers between devices: 12.9 us -> 0.02 us  [local(): block_keys = lax.all_gather(key_flat, 'ctx', axis=0, tiled=True)]
    all_gather x1, waiting for transfers between devices: 68.1 us -> 59.4 us  [local(): lax.all_gather(shards[2], 'dp', axis=0, tiled=True)]
  transfers between devices with their start and end apart: 13 -> 15, of which waited for: 11 -> 11; matrix products, arithmetic and copies ran while one was open for 14% -> 15% of each run, Pallas kernels for 0% -> 0%
where the time goes in v1:
time: 658 us
  waiting for transfers between devices  456 us (69%)
  matrix products  70.7 us (11%)
  blocking collectives  64.6 us (10%)
  other arithmetic  26.6 us (4%)
  local copies, waits for them, and re-layouts  21.6 us (3%)
  between operations  15.9 us (2%)
    reduce_scatter x1, waiting for transfers between devices, local(): lax.psum_scatter(local_grads[0].astype(jnp.bfloat16), 'dp', scatter_dimen...  69 us
    reduce_scatter x1, waiting for transfers between devices, local(): lax.psum_scatter(local_grads[2].astype(jnp.bfloat16), 'dp', scatter_dimen...  67.9 us
    ppermute x2, waiting for transfers between devices, doubled_up(): theirs = lax.ppermute(grown, axis, [(d, d ^ reach) for d in range(ways)])  67.3 us
    all_gather x1, waiting for transfers between devices, local(): lax.all_gather(shards[2], 'dp', axis=0, tiled=True)  59.4 us
    all_gather x1, waiting for transfers between devices, local(): lax.all_gather(shards[0], 'dp', axis=0, tiled=True)  53.9 us
    reduce_scatter x1, waiting for transfers between devices, local(): lax.psum_scatter(local_grads[3].astype(jnp.bfloat16), 'dp', scatter_dimen...  39.2 us
    psum x1, waiting for transfers between devices, local(): lax.psum(shares[0].astype(jnp.bfloat16), 'ctx').astype(jnp.float32)  37.9 us
    all_gather x1, waiting for transfers between devices, local(): lax.all_gather(shards[1], 'dp', axis=0, tiled=True)  36.7 us
  transfers between devices with their start and end apart: 15, of which 11 were waited for; matrix products, arithmetic and copies ran while one was open for 15% of the time, Pallas kernels for 0%

profile of v1, /device:TPU:0, one launch (start us, length us, event | category | flops | bytes accessed | tf_op | source)
XLA Modules:
  0.0 657.5 jit_solution(431908387409664196)
XLA Ops:
  11.6 13.6 %all-reduce.7 = (bf16[768]{0:T(1024)(128)(2,1)S(1)}, bf16[768]{0:T(1024)(128)(2,1)S(1)}) all-reduce(bf16[768]{0:T(1024)(128)(2,1)S(1)} %dynamic-update-slice, bf16[768]{0:T(1024)(128)(2,1)S(1)} %dynamic-update-slice.1), channel_id=1, replica_groups=mesh['dp'=4,'ctx'=8] {'dp'}, use_global_device_ids=true, to_apply=%add | all-reduce | flops 1536 | bytes 6144
  28.5 53.9 %all-gather.10.cloned.1.call-done = bf16[768,2304]{1,0:T(8,128)(2,1)} async-done(((bf16[192,2304]{1,0:T(8,128)(2,1)}), bf16[768,2304]{1,0:T(8,128)(2,1)}) %all-gather.10.cloned.1.call-update) | async-done | bytes 3538960 | tf_op jit(solution)/shard_map/all_gather | solution.py:78
  91.4 8.7 %all-gather = s32[1,1024]{1,0:T(1,128)S(1)} all-gather(s32[1,128]{1,0:T(1,128)S(1)} %copy-done.42), channel_id=2, replica_groups=mesh['dp'=4,'ctx'=8] {'ctx'}, dimensions={1}, use_global_device_ids=true | all-gather | bytes 4608 | tf_op jit(solution)/shard_map/all_gather | solution.py:104
  100.3 12.6 %collective-permute-done = bf16[192,2304]{1,0:T(8,128)(2,1)S(1)} collective-permute-done((bf16[192,2304]{1,0:T(8,128)(2,1)}, bf16[192,2304]{1,0:T(8,128)(2,1)S(1)}, u32[]{:S(2)}, u32[]{:S(2)}) %collective-permute-start) | collective-permute-done | bytes 884768 | tf_op jit(solution)/shard_map/ppermute | solution.py:16
  125.2 15.5 %all-gather.12.cloned.1.call-done = bf16[1024,768]{1,0:T(8,128)(2,1)} async-done(((bf16[128,768]{1,0:T(8,128)(2,1)}), bf16[1024,768]{1,0:T(8,128)(2,1)}) %all-gather.12.cloned.1.call-update) | async-done | bytes 1572880 | tf_op jit(solution)/shard_map/all_gather | solution.py:103
  143.3 5.8 fusion.95
  149.1 36.7 %all-gather.16.cloned.1.call-done = bf16[768,768]{1,0:T(8,128)(2,1)} async-done(((bf16[192,768]{1,0:T(8,128)(2,1)}), bf16[768,768]{1,0:T(8,128)(2,1)}) %all-gather.16.cloned.1.call-update) | async-done | bytes 1179664 | tf_op jit(solution)/shard_map/all_gather | solution.py:79
  187.8 54.7 %collective-permute-done.1 = bf16[384,2304]{1,0:T(8,128)(2,1)} collective-permute-done((bf16[384,2304]{1,0:T(8,128)(2,1)}, bf16[384,2304]{1,0:T(8,128)(2,1)}, u32[]{:S(2)}, u32[]{:S(2)}) %collective-permute-start.1) | collective-permute-done | bytes 1769504 | tf_op jit(solution)/shard_map/ppermute | solution.py:16
  242.5 5.5 fusion.3
  252.7 59.4 %all-gather.20.cloned.1.call-done = bf16[768,2304]{1,0:T(8,128)(2,1)} async-done(((bf16[192,2304]{1,0:T(8,128)(2,1)}), bf16[768,2304]{1,0:T(8,128)(2,1)}) %all-gather.20.cloned.1.call-update) | async-done | bytes 3538960 | tf_op jit(solution)/shard_map/all_gather | solution.py:143
  312.2 4.1 multiply_reduce_fusion
  332.1 6.8 %all-gather.22.cloned.1.call-done = bf16[1024,768]{1,0:T(8,128)(2,1)} async-done(((bf16[128,768]{1,0:T(8,128)(2,1)}), bf16[1024,768]{1,0:T(8,128)(2,1)}) %all-gather.22.cloned.1.call-update) | async-done | bytes 1572880 | tf_op jit(solution)/shard_map/all_gather | solution.py:190
  342.2 10.3 %all_gather.58 = f32[12,1024]{1,0:T(8,128)} all-gather(f32[12,128]{1,0:T(8,128)S(1)} %log_add_fusion), channel_id=1, replica_groups=mesh['dp'=4,'ctx'=8] {'ctx'}, dimensions={1}, use_global_device_ids=true | all-gather | bytes 55296 | tf_op jit(solution)/shard_map/all_gather | solution.py:165
  353.5 9.3 %all_gather.60 = f32[12,1024]{1,0:T(8,128)} all-gather(f32[12,128]{1,0:T(8,128)S(1)} %bitcast.130), channel_id=1, replica_groups=mesh['dp'=4,'ctx'=8] {'ctx'}, dimensions={1}, use_global_device_ids=true | all-gather | bytes 55296 | tf_op jit(solution)/shard_map/all_gather | solution.py:166
  362.8 5.2 fusion.61
  370.8 9.0 %fusion.24 = f32[128,12,64]{0,2,1:T(8,128)} fusion(bf16[1024,12,64]{0,2,1:T(8,128)(2,1)} %bitcast.104, f32[12,1024,128]{2,1,0:T(8,128)} %fusion.61, f32[12,1024]{1,0:T(8,128)S(1)} %copy-done.28, f32[12,1024]{1,0:T(8,128)S(1)} %copy-done.26, pred[1024,128]{1,0:T(8,128)(4,1)S(1)} %copy-done.24, bf16[1024,12,64]{0,2,1:T(8,128)(2,1)} %bitcast.113, ...), kind=kOutput, calls=%fused_computation.31 | convolution fusion | flops 412090368 | bytes 10256384 | tf_op jit(solution)/shard_map/hqk,qhe->khe/dot_general | solution.py:211
  379.7 7.0 %broadcast_multiply_fusion.1 = (f32[128,12,64]{0,2,1:T(8,128)S(1)}, f32[128,12,64]{0,2,1:T(8,128)}, f32[128,12,64]{0,2,1:T(8,128)}) fusion(f32[128,64]{0,1:T(8,128)} %get-tuple-element.47, f32[128,12,64]{0,2,1:T(8,128)} %fusion.24, bf16[1024,12,64]{0,2,1:T(8,128)(2,1)S(1)} %bitcast.102, f32[12,128,1024]{2,1,0:T(8,128)} %copy-done, ...), kind=kOutput, calls=%fused_computation.111 | convolution fusion | flops 412286976 | bytes 11382784 | tf_op jit(solution)/shard_map/hqk,khe->qhe/dot_general | solution.py:187
  389.3 5.0 fusion.30
  399.0 39.2 %reduce-scatter.11.cloned.1.call-done = bf16[288,768]{1,0:T(8,128)(2,1)} async-done(((bf16[1152,768]{1,0:T(8,128)(2,1)}), bf16[288,768]{1,0:T(8,128)(2,1)}) %reduce-scatter.11.cloned.1.call-update) | async-done | bytes 442384 | tf_op jit(solution)/shard_map/reduce_scatter | solution.py:239
  438.1 67.9 %reduce-scatter.9.cloned.1.call-done = bf16[192,2304]{1,0:T(8,128)(2,1)} async-done(((bf16[768,2304]{1,0:T(8,128)(2,1)}), bf16[192,2304]{1,0:T(8,128)(2,1)}) %reduce-scatter.9.cloned.1.call-update) | async-done | bytes 884752 | tf_op jit(solution)/shard_map/reduce_scatter | solution.py:236
  506.1 69.0 %reduce-scatter.5.cloned.1.call-done = bf16[192,2304]{1,0:T(8,128)(2,1)} async-done(((bf16[768,2304]{1,0:T(8,128)(2,1)}), bf16[192,2304]{1,0:T(8,128)(2,1)}) %reduce-scatter.5.cloned.1.call-update) | async-done | bytes 884752 | tf_op jit(solution)/shard_map/reduce_scatter | solution.py:230
  581.4 10.7 %all-reduce.6 = (bf16[768]{0:T(1024)(128)(2,1)S(1)}, bf16[768]{0:T(1024)(128)(2,1)S(1)}) all-reduce(bf16[768]{0:T(1024)(128)(2,1)S(1)} %get-tuple-element.10, bf16[768]{0:T(1024)(128)(2,1)S(1)} %copy-done.39), channel_id=7, replica_groups=mesh['dp'=4,'ctx'=8] {'dp'}, use_global_device_ids=true, to_apply=%region_20.21.clone | all-reduce | flops 1536 | bytes 6144
  592.3 11.9 %all-reduce.4 = (bf16[192]{0:T(256)(128)(2,1)S(1)}, bf16[192]{0:T(256)(128)(2,1)S(1)}) all-reduce(bf16[192]{0:T(256)(128)(2,1)S(1)} %dynamic-slice.3, bf16[192]{0:T(256)(128)(2,1)S(1)} %dynamic-slice.5), channel_id=1, replica_groups=mesh['dp'=4,'ctx'=8] {'ctx'}, use_global_device_ids=true, to_apply=%region_21.22 | all-reduce | flops 384 | bytes 1536 | tf_op jit(solution)/shard_map/psum | solution.py:254
  606.4 37.9 %all-reduce.10.cloned.1.call-done = (bf16[192,2304]{1,0:T(8,128)(2,1)}, bf16[192,768]{1,0:T(8,128)(2,1)}, bf16[192,2304]{1,0:T(8,128)(2,1)}, bf16[288,768]{1,0:T(8,128)(2,1)}) async-done(((bf16[192,2304]{1,0:T(8,128)(2,1)}, bf16[192,768]{1,0:T(8,128)(2,1)}, bf16[192,2304]{1,0:T(8,128)(2,1)}, bf16[288,768]{1,0:T(8,128)(2,1)}), (bf16[192,2304]{1,0:T(8,128)(2,1)}, bf16[192,768]{1,0:T(8,128)(2,1)}, ...) | async-done | bytes 2506768 | tf_op jit(solution)/shard_map/psum | solution.py:250
  (203 shorter events, 81.9 us)
Async XLA Ops:
  7.2 75.2 %all-gather.10.cloned.1.call-start = ((), (), s32[]{:S(2)}) async-start(), calls=%async_computation.4 | async-start | bytes 4423680 | tf_op jit(solution)/shard_map/all_gather | solution.py:78
  7.9 109.6 %all-gather.14.cloned.1.call-start = ((), (), s32[]{:S(2)}) async-start(), calls=%async_computation.6 | async-start | bytes 1769472 | tf_op jit(solution)/shard_map/all_gather | solution.py:102
  26.0 56.3 %copy-start.18 = (f32[128,64]{0,1:T(8,128)}, f32[128,64]{0,1:T(8,128)S(1)}, u32[]{:S(2)}) copy-start(f32[128,64]{0,1:T(8,128)S(1)} %get-tuple-element.49) | copy-start | bytes 98308
  88.7 52.1 %all-gather.12.cloned.1.call-start = ((), (), s32[]{:S(2)}) async-start(), calls=%async_computation.5 | async-start | bytes 1769472 | tf_op jit(solution)/shard_map/all_gather | solution.py:103
  89.4 96.4 %all-gather.16.cloned.1.call-start = ((), (), s32[]{:S(2)}) async-start(), calls=%async_computation.7 | async-start | bytes 1474560 | tf_op jit(solution)/shard_map/all_gather | solution.py:79
  90.0 158.0 %all-gather.18.cloned.1.call-start = ((), (), s32[]{:S(2)}) async-start(), calls=%async_computation.8 | async-start | bytes 2211840 | tf_op jit(solution)/shard_map/all_gather | solution.py:81
  90.6 221.5 %all-gather.20.cloned.1.call-start = ((), (), s32[]{:S(2)}) async-start(), calls=%async_computation.9 | async-start | bytes 4423680 | tf_op jit(solution)/shard_map/all_gather | solution.py:143
  91.2 247.7 %all-gather.22.cloned.1.call-start = ((), (), s32[]{:S(2)}) async-start(), calls=%async_computation.10 | async-start | bytes 1769472 | tf_op jit(solution)/shard_map/all_gather | solution.py:190
  91.2 21.6 %collective-permute-start = (bf16[192,2304]{1,0:T(8,128)(2,1)}, bf16[192,2304]{1,0:T(8,128)(2,1)S(1)}, u32[]{:S(2)}, u32[]{:S(2)}) collective-permute-start(bf16[192,2304]{1,0:T(8,128)(2,1)} %param.13), channel_id=1, source_target_pairs={{0,8},{8,0},{16,24},{24,16},{1,9},{9,1},{17,25},{25,17},{2,10},{10... | collective-permute-start | bytes 2654216 | tf_op jit(solution)/shard_map/ppermute | solution.py:16
  116.2 126.3 %collective-permute-start.1 = (bf16[384,2304]{1,0:T(8,128)(2,1)}, bf16[384,2304]{1,0:T(8,128)(2,1)}, u32[]{:S(2)}, u32[]{:S(2)}) collective-permute-start(bf16[384,2304]{1,0:T(8,128)(2,1)} %maximum_select_fusion.2), channel_id=1, source_target_pairs={{0,16},{8,24},{16,0},{24,8},{1,17},{9,25},{17,1},{25,9},{2,18},{10... | collective-permute-start | bytes 5308424 | tf_op jit(solution)/shard_map/ppermute | solution.py:16
  117.3 250.8 %all-gather.24.cloned.1.call-start = ((), (), s32[]{:S(2)}) async-start(), calls=%async_computation.11 | async-start | bytes 1769472 | tf_op jit(solution)/shard_map/all_gather | solution.py:191
  187.5 60.5 %copy-start.37 = (f32[128]{0:T(128)}, f32[128]{0:T(128)S(1)}, u32[]{:S(2)}) copy-start(f32[128]{0:T(128)S(1)} %broadcast_multiply_fusion.5) | copy-start | bytes 1540
  187.7 60.3 %copy-start.47 = (f32[128]{0:T(128)}, f32[128]{0:T(128)S(1)}, u32[]{:S(2)}) copy-start(f32[128]{0:T(128)S(1)} %multiply_reduce_fusion.3) | copy-start | bytes 1540
  187.8 60.2 %copy-start.40 = (f32[128]{0:T(128)}, f32[128]{0:T(128)S(1)}, u32[]{:S(2)}) copy-start(f32[128]{0:T(128)S(1)} %fusion.70) | copy-start | bytes 1540
  187.8 60.3 %copy-start.8 = (bf16[1,128,768]{2,1,0:T(8,128)(2,1)S(1)}, bf16[1,128,768]{2,1,0:T(8,128)(2,1)}, u32[]{:S(2)}) copy-start(bf16[1,128,768]{2,1,0:T(8,128)(2,1)} %param.17) | copy-start | bytes 589828
  251.9 64.4 %copy-start.14 = (bf16[128,1152]{1,0:T(8,128)(2,1)}, bf16[128,1152]{1,0:T(8,128)(2,1)S(1)}, u32[]{:S(2)}) copy-start(bf16[128,1152]{1,0:T(8,128)(2,1)S(1)} %get-tuple-element.24) | copy-start | bytes 884740
  252.7 63.6 %copy-start.5 = (bf16[128,1152]{1,0:T(8,128)(2,1)}, bf16[128,1152]{1,0:T(8,128)(2,1)S(1)}, u32[]{:S(2)}) copy-start(bf16[128,1152]{1,0:T(8,128)(2,1)S(1)} %get-tuple-element.26) | copy-start | bytes 884740
  318.5 80.5 %reduce-scatter.7.cloned.1.call-start = ((), (), s32[]{:S(2)}) async-start(), calls=%async_computation.13 | async-start | bytes 1474560 | tf_op jit(solution)/shard_map/reduce_scatter | solution.py:233
  320.9 117.2 %reduce-scatter.11.cloned.1.call-start = ((), (), s32[]{:S(2)}) async-start(), calls=%async_computation.15 | async-start | bytes 2211840 | tf_op jit(solution)/shard_map/reduce_scatter | solution.py:239
  323.9 182.2 %reduce-scatter.9.cloned.1.call-start = ((), (), s32[]{:S(2)}) async-start(), calls=%async_computation.14 | async-start | bytes 4423680 | tf_op jit(solution)/shard_map/reduce_scatter | solution.py:236
  328.0 247.0 %reduce-scatter.5.cloned.1.call-start = ((), (), s32[]{:S(2)}) async-start(), calls=%async_computation.12 | async-start | bytes 4423680 | tf_op jit(solution)/shard_map/reduce_scatter | solution.py:230
  397.9 177.1 %copy-start.6 = (bf16[128,1152]{1,0:T(8,128)(2,1)S(1)}, bf16[128,1152]{1,0:T(8,128)(2,1)}, u32[]{:S(2)}) copy-start(bf16[128,1152]{1,0:T(8,128)(2,1)} %get-tuple-element.27) | copy-start | bytes 884740
  398.0 179.7 %copy-start.22 = (bf16[12,64,128]{2,1,0:T(8,128)(2,1)S(1)}, bf16[12,64,128]{2,1,0:T(8,128)(2,1)}, u32[]{:S(2)}) copy-start(bf16[12,64,128]{2,1,0:T(8,128)(2,1)} %copy-done.21) | copy-start | bytes 589828
  398.0 246.3 %all-reduce.10.cloned.1.call-start = ((), (), s32[]{:S(2)}) async-start(), calls=%async_computation.16 | async-start | bytes 5013504 | tf_op jit(solution)/shard_map/psum | solution.py:250
  (40 other events, 538.2 us)
Sparse Core Ops, SparseCore 0:
  9.6 72.7 all-gather.9
  88.8 24.2 all-gather.13
  115.0 25.7 all-gather.11
  142.2 43.5 all-gather.15
  187.2 54.5 all-gather.17
  243.2 68.8 all-gather.19
  314.6 24.2 all-gather.21
  340.8 25.8 all-gather.23
  369.1 29.1 reduce-scatter.6
  401.0 37.0 reduce-scatter.10
  440.6 65.4 reduce-scatter.8
  508.4 66.6 reduce-scatter.4
  579.2 65.0 all-reduce.9
